TPU v7x, 512 devices: a whole 4x8x8 slice. The times are simulated.
512 devices in a mesh: band: 128 (over z, y_lo, x, core), head: 4 (over y_hi).
Axes of the slice: x: 4, y: 8 (y_hi: 4, y_lo: 2; y = y_hi * 2 + y_lo), z: 8, core: 2. Of those that a mesh axis runs over, the one named last changes fastest.
Arguments:
- queries: bfloat16 [16384, 1536], P('band', 'head'), as said below
- keys: bfloat16 [16384, 1536], P('band', 'head'), as said below
- values: bfloat16 [16384, 1536], P('band', 'head'), may hold values from -6 to 6
- d_out: bfloat16 [16384, 1536], P('band', 'head'), may hold values from -6 to 6
- gain: float32 [1536], P('head'), may hold values from 0.1 to 1.9
- blocks_on: int32 [128, 4], P('band'), may hold values 0 or 1
Outputs:
- out: bfloat16 [16384, 1536], P('band', 'head')
- d_queries: bfloat16 [16384, 1536], P('band', 'head')
- d_keys: bfloat16 [16384, 1536], P('band', 'head')
- d_values: bfloat16 [16384, 1536], P('band', 'head')
Inputs may be any that keep to these rules, and one draw needn't show every extreme that they name: `queries`: entries lie within -180 to 180. `keys`: entries lie within -6 to 6.
All inputs are finite; a program needn't handle non-finite values. No bound on the sum of `blocks_on` on one device may be relied on, other than what follows from the above.
Results may differ from a plain program's by a relative error of at most 0.0063.
Values may be sent and summed in bfloat16 or wider, within the bound.
A program may use at most 64 MiB of HBM per device.

v0:
```python
import jax
import jax.numpy as jnp
from jax import lax
from jax.sharding import PartitionSpec as P

HEAD_DIM = 128
NEG = -1e30
EPS = 1e-06


def from_behind(array, axis, by):
    devices = lax.axis_size(axis)
    pairs = [(i, i + by) for i in range(devices) if 0 <= i + by < devices]
    return lax.ppermute(array, axis, pairs)


def row_pairs_matrix(left, right):
    return lax.dot_general(
        left, right, (((1,), (1,)), ((), ())), preferred_element_type=jnp.float32
    )


def cols_by_cols(left, right):
    return lax.dot_general(
        left, right, (((0,), (0,)), ((), ())), preferred_element_type=jnp.float32
    )


def product(left, right):
    return jnp.dot(left, right, preferred_element_type=jnp.float32)


def one_head(matrix, head_index):
    return matrix[:, head_index * HEAD_DIM : (head_index + 1) * HEAD_DIM]


def local(queries, keys, values, d_out, gain, blocks_on):
    row_count = queries.shape[0]
    heads_here = queries.shape[1] // HEAD_DIM
    blocks = lax.axis_size("band")
    spacing = blocks // 8
    block_offsets = [-2 * spacing, -spacing, spacing, 2 * spacing]
    position = lax.axis_index("band")
    scaling = HEAD_DIM ** (-0.5)
    full_width = queries.shape[1] * lax.axis_size("head")
    key_value = jnp.stack([keys, values])
    reached = [key_value]
    allowed = [jnp.ones((), jnp.bool_)]
    for slot_index, offset in enumerate(block_offsets):
        reached.append(from_behind(key_value, "band", -offset))
        target = position + offset
        allowed.append((target >= 0) & (target < blocks) & (blocks_on[0, slot_index] == 1))
    gathered = jnp.concatenate(reached, axis=1)
    key_all = gathered[0]
    value_all = gathered[1]
    column_ok = jnp.repeat(jnp.stack(allowed), row_count)

    def scores(head_index):
        raw_score = (
            row_pairs_matrix(one_head(queries, head_index), one_head(key_all, head_index)) * scaling
        )
        return jnp.where(column_ok[None, :], raw_score, NEG)

    peaks, totals, pieces = ([], [], [])
    for head_index in range(heads_here):
        score = scores(head_index)
        peak = jnp.max(score, axis=1)
        exponent = jnp.exp(score - peak[:, None])
        total = jnp.sum(exponent, axis=1)
        weight_probs = (exponent / total[:, None]).astype(jnp.bfloat16)
        pieces.append(product(weight_probs, one_head(value_all, head_index)).astype(jnp.bfloat16))
        peaks.append(peak)
        totals.append(total)
    attention = jnp.concatenate(pieces, axis=1)
    attention_wide = attention.astype(jnp.float32)
    square_sum = lax.psum(jnp.sum(attention_wide * attention_wide, axis=1), "head")
    inverse = lax.rsqrt(square_sum / full_width + EPS)
    out = (attention_wide * inverse[:, None] * gain).astype(jnp.bfloat16)
    gradient_pass = d_out.astype(jnp.float32) * gain
    along = lax.psum(jnp.sum(gradient_pass * attention_wide, axis=1), "head")
    d_attn = (
        inverse[:, None] * gradient_pass
        - attention_wide * (inverse**3 * along / full_width)[:, None]
    ).astype(jnp.bfloat16)
    deltas = [
        jnp.sum(
            one_head(d_attn, head_index).astype(jnp.float32) * one_head(attention_wide, head_index),
            axis=1,
        )
        for head_index in range(heads_here)
    ]
    query_parts, key_parts, value_parts = ([], [], [])
    for head_index in range(heads_here):
        score = scores(head_index)
        probs = jnp.exp(score - peaks[head_index][:, None]) / totals[head_index][:, None]
        upstream = one_head(d_attn, head_index)
        d_weights = row_pairs_matrix(upstream, one_head(value_all, head_index))
        d_score = (probs * (d_weights - deltas[head_index][:, None])).astype(jnp.bfloat16)
        query_parts.append(product(d_score, one_head(key_all, head_index)) * scaling)
        weight_probs = probs.astype(jnp.bfloat16)
        key_parts.append(cols_by_cols(d_score, one_head(queries, head_index)) * scaling)
        value_parts.append(cols_by_cols(weight_probs, upstream))
    d_queries = jnp.concatenate(query_parts, axis=1).astype(jnp.bfloat16)
    stacked_grads = jnp.stack(
        [jnp.concatenate(key_parts, axis=1), jnp.concatenate(value_parts, axis=1)]
    )
    summed = stacked_grads[:, :row_count]
    for slot_index, offset in enumerate(block_offsets):
        outgoing = stacked_grads[
            :, (slot_index + 1) * row_count : (slot_index + 2) * row_count
        ].astype(jnp.bfloat16)
        arrived = from_behind(outgoing, "band", offset)
        summed = summed + arrived.astype(jnp.float32)
    d_keys = summed[0].astype(jnp.bfloat16)
    d_values = summed[1].astype(jnp.bfloat16)
    return (out, d_queries, d_keys, d_values)


def solution(mesh):
    in_specs = (
        P("band", "head"),
        P("band", "head"),
        P("band", "head"),
        P("band", "head"),
        P("head"),
        P("band", None),
    )
    out_specs = (P("band", "head"), P("band", "head"), P("band", "head"), P("band", "head"))
    return jax.shard_map(local, mesh=mesh, in_specs=in_specs, out_specs=out_specs, check_vma=False)
```

profile of v0, /device:TPU:6, one launch (start us, length us, event | category | flops | bytes accessed | tf_op | source)
XLA Modules:
  0.0 70.1 jit_solution(15155738258795446889)
XLA Ops:
  0.6 1.0 %pad_maximum_fusion.1 = (bf16[2,128,384]{2,1,0:T(8,128)(2,1)S(1)}, bf16[2,640,384]{2,1,0:T(8,128)(2,1)S(1)}) fusion(bf16[1,128,384]{2,1,0:T(8,128)(2,1)} %bitcast.45, bf16[1,128,384]{2,1,0:T(8,128)(2,1)} %bitcast.46), kind=kLoop, calls=%fused_computation.53 | loop fusion | flops 393215 | bytes 589824 | tf_op jit(solution)/shard_map/stack | solution.py:46
  1.6 1.3 %collective-permute-start.2 = (bf16[2,128,384]{2,1,0:T(8,128)(2,1)S(1)}, bf16[2,128,384]{2,1,0:T(8,128)(2,1)S(1)}, u32[]{:S(2)}, u32[]{:S(2)}) collective-permute-start(bf16[2,128,384]{2,1,0:T(8,128)(2,1)S(1)} %get-tuple-element.23), channel_id=1, source_target_pairs={{64,0},{68,4},{72,8},{76,12},{80,16},{84,20},{88,24},{92,28},{96,3... | collective-permute-start | bytes 589832 | tf_op jit(solution)/shard_map/ppermute | solution.py:14
  2.9 4.9 %collective-permute-start.1 = (bf16[2,128,384]{2,1,0:T(8,128)(2,1)S(1)}, bf16[2,128,384]{2,1,0:T(8,128)(2,1)S(1)}, u32[]{:S(2)}, u32[]{:S(2)}) collective-permute-start(bf16[2,128,384]{2,1,0:T(8,128)(2,1)S(1)} %get-tuple-element.23), channel_id=1, source_target_pairs={{0,64},{4,68},{8,72},{12,76},{16,80},{20,84},{24,88},{28,92},{32,9... | collective-permute-start | bytes 589832 | tf_op jit(solution)/shard_map/ppermute | solution.py:14
  7.8 6.1 %collective-permute-start = (bf16[2,128,384]{2,1,0:T(8,128)(2,1)S(1)}, bf16[2,128,384]{2,1,0:T(8,128)(2,1)S(1)}, u32[]{:S(2)}, u32[]{:S(2)}) collective-permute-start(bf16[2,128,384]{2,1,0:T(8,128)(2,1)S(1)} %get-tuple-element.23), channel_id=1, source_target_pairs={{0,128},{4,132},{8,136},{12,140},{16,144},{20,148},{24,152},{28,15... | collective-permute-start | bytes 589832 | tf_op jit(solution)/shard_map/ppermute | solution.py:14
  13.9 1.3 %collective-permute-start.3 = (bf16[2,128,384]{2,1,0:T(8,128)(2,1)S(1)}, bf16[2,128,384]{2,1,0:T(8,128)(2,1)S(1)}, u32[]{:S(2)}, u32[]{:S(2)}) collective-permute-start(bf16[2,128,384]{2,1,0:T(8,128)(2,1)S(1)} %get-tuple-element.23), channel_id=1, source_target_pairs={{128,0},{132,4},{136,8},{140,12},{144,16},{148,20},{152,24},{156,2... | collective-permute-start | bytes 589832 | tf_op jit(solution)/shard_map/ppermute | solution.py:14
  15.2 1.4 %fusion.59 = (s32[1,1]{1,0:T(1,128)}, s32[1,1]{1,0:T(1,128)}, s32[1,1]{1,0:T(1,128)}, s32[1,1]{1,0:T(1,128)}) fusion(s32[1,4]{1,0:T(1,128)} %param.11), kind=kLoop, calls=%fused_computation.108 | loop fusion | bytes 32 | tf_op jit(solution)/shard_map/slice | solution.py:52
  19.3 0.1 stack.37
  19.4 0.1 broadcast_bitcast_fusion
  19.5 1.0 %copy.10 = bf16[128,384]{0,1:T(8,128)(2,1)S(1)} copy(bf16[128,384]{1,0:T(8,128)(2,1)} %param.9) | data formatting | bytes 196608 | tf_op args[3]
  20.6 8.5 %collective-permute-done.3 = bf16[2,128,384]{2,1,0:T(8,128)(2,1)S(1)} collective-permute-done((bf16[2,128,384]{2,1,0:T(8,128)(2,1)S(1)}, bf16[2,128,384]{2,1,0:T(8,128)(2,1)S(1)}, u32[]{:S(2)}, u32[]{:S(2)}) %collective-permute-start.3) | collective-permute-done | bytes 196640 | tf_op jit(solution)/shard_map/ppermute | solution.py:14
  29.2 0.1 slice_bitcast_fusion
  29.3 0.8 %copy-done = bf16[128,384]{1,0:T(8,128)(2,1)S(1)} copy-done((bf16[128,384]{1,0:T(8,128)(2,1)S(1)}, bf16[128,384]{1,0:T(8,128)(2,1)}, u32[]{:S(2)}) %copy-start) | copy-done | bytes 98328
  30.1 0.3 fusion.60
  30.3 0.3 fusion.61
  30.6 0.3 fusion.62
  30.9 0.1 fusion.23
  31.0 0.1 fusion.21
  31.2 0.3 convolution_convert_fusion
  31.5 0.3 convolution_convert_fusion.1
  31.8 0.1 fusion.19
  32.0 0.3 convolution_convert_fusion.2
  32.3 0.1 multiply_reduce_fusion
  32.4 12.9 %all-reduce = (f32[128]{0:T(128)S(1)}, f32[128]{0:T(128)S(1)}) all-reduce(f32[128]{0:T(128)S(1)} %get-tuple-element.12, f32[128]{0:T(128)S(1)} %get-tuple-element.11), channel_id=1, replica_groups=mesh['band'=128,'head'=4] {'head'}, use_global_device_ids=true, to_apply=%region_7.8 | all-reduce | flops 256 | bytes 2048 | tf_op jit(solution)/shard_map/psum | solution.py:76
  45.3 0.1 subtract_convert_fusion
  45.5 0.2 fusion.8
  45.7 0.3 fusion.11
  45.9 0.2 convolution_multiply_fusion.1
  46.1 0.2 fusion.7
  46.3 0.3 fusion.10
  46.6 0.2 convolution_multiply_fusion.2
  46.8 0.2 fusion.49
  47.0 0.2 fusion.52
  47.2 0.2 fusion.46
  47.4 0.2 fusion.9
  47.6 0.2 convolution_multiply_fusion
  47.8 0.1 maximum_bitcast_fusion
  47.9 0.2 fusion
  48.1 0.8 %fusion.58 = (bf16[2,128,384]{2,1,0:T(8,128)(2,1)}, bf16[2,128,384]{2,1,0:T(8,128)(2,1)}, bf16[2,128,384]{2,1,0:T(8,128)(2,1)S(1)}, bf16[2,128,384]{2,1,0:T(8,128)(2,1)S(1)}) fusion(bf16[2,640,384]{2,1,0:T(8,128)(2,1)S(1)} %fusion), kind=kLoop, calls=%fused_computation.107 | loop fusion | bytes 1572864 | tf_op jit(solution)/shard_map/slice | solution.py:109
  48.9 1.3 %collective-permute-start.4 = (bf16[2,128,384]{2,1,0:T(8,128)(2,1)}, bf16[2,128,384]{2,1,0:T(8,128)(2,1)S(1)}, u32[]{:S(2)}, u32[]{:S(2)}) collective-permute-start(bf16[2,128,384]{2,1,0:T(8,128)(2,1)} %get-tuple-element.15), channel_id=1, source_target_pairs={{128,0},{132,4},{136,8},{140,12},{144,16},{148,20},{152,24},{156,2... | collective-permute-start | bytes 589832 | tf_op jit(solution)/shard_map/ppermute | solution.py:14
  50.2 5.5 %collective-permute-start.7 = (bf16[2,128,384]{2,1,0:T(8,128)(2,1)}, bf16[2,128,384]{2,1,0:T(8,128)(2,1)S(1)}, u32[]{:S(2)}, u32[]{:S(2)}) collective-permute-start(bf16[2,128,384]{2,1,0:T(8,128)(2,1)} %get-tuple-element.16), channel_id=1, source_target_pairs={{0,128},{4,132},{8,136},{12,140},{16,144},{20,148},{24,152},{28,15... | collective-permute-start | bytes 589832 | tf_op jit(solution)/shard_map/ppermute | solution.py:14
  55.7 5.0 %collective-permute-start.6 = (bf16[2,128,384]{2,1,0:T(8,128)(2,1)S(1)}, bf16[2,128,384]{2,1,0:T(8,128)(2,1)}, u32[]{:S(2)}, u32[]{:S(2)}) collective-permute-start(bf16[2,128,384]{2,1,0:T(8,128)(2,1)S(1)} %get-tuple-element.17), channel_id=1, source_target_pairs={{0,64},{4,68},{8,72},{12,76},{16,80},{20,84},{24,88},{28,92},{32,9... | collective-permute-start | bytes 589832 | tf_op jit(solution)/shard_map/ppermute | solution.py:14
  60.6 1.3 %collective-permute-start.5 = (bf16[2,128,384]{2,1,0:T(8,128)(2,1)S(1)}, bf16[2,128,384]{2,1,0:T(8,128)(2,1)}, u32[]{:S(2)}, u32[]{:S(2)}) collective-permute-start(bf16[2,128,384]{2,1,0:T(8,128)(2,1)S(1)} %get-tuple-element.18), channel_id=1, source_target_pairs={{64,0},{68,4},{72,8},{76,12},{80,16},{84,20},{88,24},{92,28},{96,3... | collective-permute-start | bytes 589832 | tf_op jit(solution)/shard_map/ppermute | solution.py:14
  61.9 0.3 fusion.12
  62.2 0.8 %copy.20 = bf16[128,384]{1,0:T(8,128)(2,1)} copy(bf16[128,384]{0,1:T(8,128)(2,1)S(1)} %get-tuple-element.26) | data formatting | bytes 196608
  63.0 0.8 %copy.21 = bf16[128,384]{1,0:T(8,128)(2,1)} copy(bf16[128,384]{0,1:T(8,128)(2,1)S(1)} %pad_maximum_fusion.3) | data formatting | bytes 196608
  63.7 4.6 %collective-permute-done.5 = bf16[2,128,384]{2,1,0:T(8,128)(2,1)} collective-permute-done((bf16[2,128,384]{2,1,0:T(8,128)(2,1)S(1)}, bf16[2,128,384]{2,1,0:T(8,128)(2,1)}, u32[]{:S(2)}, u32[]{:S(2)}) %collective-permute-start.5) | collective-permute-done | bytes 196640 | tf_op jit(solution)/shard_map/ppermute | solution.py:14
  68.3 1.1 %fusion.18 = bf16[2,128,384]{2,1,0:T(8,128)(2,1)S(1)} fusion(f32[1,640,384]{2,1,0:T(8,128)S(1)} %get-tuple-element.39, f32[1,640,384]{2,1,0:T(8,128)S(1)} %get-tuple-element.40, bf16[2,128,384]{2,1,0:T(8,128)(2,1)S(1)} %collective-permute-done.7, bf16[2,128,384]{2,1,0:T(8,128)(2,1)} %collective-permute-done.6, ...), kind=kLoop, calls=%fused_computation.40 | loop fusion | flops 983040 | bytes 2949120 | tf_op jit(solution)/shard_map/convert.1
  69.4 0.7 slice_bitcast_fusion.2
  (20 shorter events, 0.4 us)
Async XLA Ops:
  1.6 19.0 %collective-permute-start.2 = (bf16[2,128,384]{2,1,0:T(8,128)(2,1)S(1)}, bf16[2,128,384]{2,1,0:T(8,128)(2,1)S(1)}, u32[]{:S(2)}, u32[]{:S(2)}) collective-permute-start(bf16[2,128,384]{2,1,0:T(8,128)(2,1)S(1)} %get-tuple-element.23), channel_id=1, source_target_pairs={{64,0},{68,4},{72,8},{76,12},{80,16},{84,20},{88,24},{92,28},{96,3... | collective-permute-start | bytes 589832 | tf_op jit(solution)/shard_map/ppermute | solution.py:14
  2.9 17.6 %collective-permute-start.1 = (bf16[2,128,384]{2,1,0:T(8,128)(2,1)S(1)}, bf16[2,128,384]{2,1,0:T(8,128)(2,1)S(1)}, u32[]{:S(2)}, u32[]{:S(2)}) collective-permute-start(bf16[2,128,384]{2,1,0:T(8,128)(2,1)S(1)} %get-tuple-element.23), channel_id=1, source_target_pairs={{0,64},{4,68},{8,72},{12,76},{16,80},{20,84},{24,88},{28,92},{32,9... | collective-permute-start | bytes 589832 | tf_op jit(solution)/shard_map/ppermute | solution.py:14
  7.8 12.6 %collective-permute-start = (bf16[2,128,384]{2,1,0:T(8,128)(2,1)S(1)}, bf16[2,128,384]{2,1,0:T(8,128)(2,1)S(1)}, u32[]{:S(2)}, u32[]{:S(2)}) collective-permute-start(bf16[2,128,384]{2,1,0:T(8,128)(2,1)S(1)} %get-tuple-element.23), channel_id=1, source_target_pairs={{0,128},{4,132},{8,136},{12,140},{16,144},{20,148},{24,152},{28,15... | collective-permute-start | bytes 589832 | tf_op jit(solution)/shard_map/ppermute | solution.py:14
  13.9 15.2 %collective-permute-start.3 = (bf16[2,128,384]{2,1,0:T(8,128)(2,1)S(1)}, bf16[2,128,384]{2,1,0:T(8,128)(2,1)S(1)}, u32[]{:S(2)}, u32[]{:S(2)}) collective-permute-start(bf16[2,128,384]{2,1,0:T(8,128)(2,1)S(1)} %get-tuple-element.23), channel_id=1, source_target_pairs={{128,0},{132,4},{136,8},{140,12},{144,16},{148,20},{152,24},{156,2... | collective-permute-start | bytes 589832 | tf_op jit(solution)/shard_map/ppermute | solution.py:14
  29.2 0.9 %copy-start = (bf16[128,384]{1,0:T(8,128)(2,1)S(1)}, bf16[128,384]{1,0:T(8,128)(2,1)}, u32[]{:S(2)}) copy-start(bf16[128,384]{1,0:T(8,128)(2,1)} %param.6) | copy-start | bytes 294916
  31.5 0.8 %copy-start.1 = (f32[384]{0:T(512)S(1)}, f32[384]{0:T(512)}, u32[]{:S(2)}) copy-start(f32[384]{0:T(512)} %param.10) | copy-start | bytes 4612
  48.9 14.8 %collective-permute-start.4 = (bf16[2,128,384]{2,1,0:T(8,128)(2,1)}, bf16[2,128,384]{2,1,0:T(8,128)(2,1)S(1)}, u32[]{:S(2)}, u32[]{:S(2)}) collective-permute-start(bf16[2,128,384]{2,1,0:T(8,128)(2,1)} %get-tuple-element.15), channel_id=1, source_target_pairs={{128,0},{132,4},{136,8},{140,12},{144,16},{148,20},{152,24},{156,2... | collective-permute-start | bytes 589832 | tf_op jit(solution)/shard_map/ppermute | solution.py:14
  50.2 13.5 %collective-permute-start.7 = (bf16[2,128,384]{2,1,0:T(8,128)(2,1)}, bf16[2,128,384]{2,1,0:T(8,128)(2,1)S(1)}, u32[]{:S(2)}, u32[]{:S(2)}) collective-permute-start(bf16[2,128,384]{2,1,0:T(8,128)(2,1)} %get-tuple-element.16), channel_id=1, source_target_pairs={{0,128},{4,132},{8,136},{12,140},{16,144},{20,148},{24,152},{28,15... | collective-permute-start | bytes 589832 | tf_op jit(solution)/shard_map/ppermute | solution.py:14
  55.7 8.0 %collective-permute-start.6 = (bf16[2,128,384]{2,1,0:T(8,128)(2,1)S(1)}, bf16[2,128,384]{2,1,0:T(8,128)(2,1)}, u32[]{:S(2)}, u32[]{:S(2)}) collective-permute-start(bf16[2,128,384]{2,1,0:T(8,128)(2,1)S(1)} %get-tuple-element.17), channel_id=1, source_target_pairs={{0,64},{4,68},{8,72},{12,76},{16,80},{20,84},{24,88},{28,92},{32,9... | collective-permute-start | bytes 589832 | tf_op jit(solution)/shard_map/ppermute | solution.py:14
  60.6 7.7 %collective-permute-start.5 = (bf16[2,128,384]{2,1,0:T(8,128)(2,1)S(1)}, bf16[2,128,384]{2,1,0:T(8,128)(2,1)}, u32[]{:S(2)}, u32[]{:S(2)}) collective-permute-start(bf16[2,128,384]{2,1,0:T(8,128)(2,1)S(1)} %get-tuple-element.18), channel_id=1, source_target_pairs={{64,0},{68,4},{72,8},{76,12},{80,16},{84,20},{88,24},{92,28},{96,3... | collective-permute-start | bytes 589832 | tf_op jit(solution)/shard_map/ppermute | solution.py:14
where the time goes:
time: 70.6 us; the launch traced here: 70.1 us
  starting transfers between devices  26.6 us (38%)
  waiting for transfers between devices  13.1 us (19%)
  blocking collectives  12.9 us (18%)
  local copies, waits for them, and re-layouts  6.63 us (9%)
  matrix products  4.15 us (6%)
  between operations  3.56 us (5%)
  other arithmetic  3.26 us (5%)
    ppermute x8, starting transfers between devices, from_behind(): return lax.ppermute(array, axis, pairs)  26.6 us
    ppermute x8, waiting for transfers between devices, from_behind(): return lax.ppermute(array, axis, pairs)  13.1 us
    psum x1, blocking collectives, local(): lax.psum(jnp.sum(attention_wide * attention_wide, axis=1), 'head')  12.9 us
    unnamed x10, local copies, waits for them, and re-layouts  3.4 us
    dot_general x6, matrix products, product(): return jnp.dot(left, right, preferred_element_type=jnp.float32)  1.61 us
  transfers between devices with their start and end apart: 8, of which 2 were waited for; matrix products, arithmetic and copies ran while one was open for 6% of the time, Pallas kernels for 0%

commit v1 on v0

--- a/solution.py
+++ b/solution.py
@@ -73,7 +73,9 @@
         totals.append(total)
     attention = jnp.concatenate(pieces, axis=1)
     attention_wide = attention.astype(jnp.float32)
-    square_sum = lax.psum(jnp.sum(attention_wide * attention_wide, axis=1), "head")
+    part = jnp.sum(attention_wide * attention_wide, axis=1)
+    parts = lax.all_gather(part, "head")
+    square_sum = jnp.sum(parts, axis=0)
     inverse = lax.rsqrt(square_sum / full_width + EPS)
     out = (attention_wide * inverse[:, None] * gain).astype(jnp.bfloat16)
     gradient_pass = d_out.astype(jnp.float32) * gain

time: 70.6 us -> 80.6 us (1.14)
  blocking collectives: 12.9 us -> 22.8 us
    all_gather x0 -> x1, blocking collectives: none -> 9.93 us  [local(): parts = lax.all_gather(part, 'head')]
where the time goes in v1:
time: 80.6 us; the launch traced here: 80.1 us
  starting transfers between devices  26.6 us (33%)
  blocking collectives  22.8 us (28%)
  waiting for transfers between devices  13.1 us (16%)
  local copies, waits for them, and re-layouts  6.63 us (8%)
  matrix products  4.15 us (5%)
  between operations  3.56 us (4%)
  other arithmetic  3.28 us (4%)
    ppermute x8, starting transfers between devices, from_behind(): return lax.ppermute(array, axis, pairs)  26.6 us
    ppermute x8, waiting for transfers between devices, from_behind(): return lax.ppermute(array, axis, pairs)  13.1 us
    psum x1, blocking collectives, local(): along = lax.psum(jnp.sum(gradient_pass * attention_wide, axis=1), 'head')  12.9 us
    all_gather x1, blocking collectives, local(): parts = lax.all_gather(part, 'head')  9.93 us
    unnamed x10, local copies, waits for them, and re-layouts  3.4 us
    dot_general x6, matrix products, product(): return jnp.dot(left, right, preferred_element_type=jnp.float32)  1.61 us
  transfers between devices with their start and end apart: 8, of which 2 were waited for; matrix products, arithmetic and copies ran while one was open for 6% of the time, Pallas kernels for 0%

profile of v1, /device:TPU:6, one launch (start us, length us, event | category | flops | bytes accessed | tf_op | source)
XLA Modules:
  0.0 80.1 jit_solution(3968794315789168978)
XLA Ops:
  0.6 1.0 %pad_maximum_fusion.1 = (bf16[2,128,384]{2,1,0:T(8,128)(2,1)S(1)}, bf16[2,640,384]{2,1,0:T(8,128)(2,1)S(1)}) fusion(bf16[1,128,384]{2,1,0:T(8,128)(2,1)} %bitcast.46, bf16[1,128,384]{2,1,0:T(8,128)(2,1)} %bitcast.47), kind=kLoop, calls=%fused_computation.53 | loop fusion | flops 393215 | bytes 589824 | tf_op jit(solution)/shard_map/stack | solution.py:46
  1.6 1.3 %collective-permute-start.2 = (bf16[2,128,384]{2,1,0:T(8,128)(2,1)S(1)}, bf16[2,128,384]{2,1,0:T(8,128)(2,1)S(1)}, u32[]{:S(2)}, u32[]{:S(2)}) collective-permute-start(bf16[2,128,384]{2,1,0:T(8,128)(2,1)S(1)} %get-tuple-element.25), channel_id=1, source_target_pairs={{64,0},{68,4},{72,8},{76,12},{80,16},{84,20},{88,24},{92,28},{96,3... | collective-permute-start | bytes 589832 | tf_op jit(solution)/shard_map/ppermute | solution.py:14
  2.9 4.9 %collective-permute-start.1 = (bf16[2,128,384]{2,1,0:T(8,128)(2,1)S(1)}, bf16[2,128,384]{2,1,0:T(8,128)(2,1)S(1)}, u32[]{:S(2)}, u32[]{:S(2)}) collective-permute-start(bf16[2,128,384]{2,1,0:T(8,128)(2,1)S(1)} %get-tuple-element.25), channel_id=1, source_target_pairs={{0,64},{4,68},{8,72},{12,76},{16,80},{20,84},{24,88},{28,92},{32,9... | collective-permute-start | bytes 589832 | tf_op jit(solution)/shard_map/ppermute | solution.py:14
  7.8 6.1 %collective-permute-start = (bf16[2,128,384]{2,1,0:T(8,128)(2,1)S(1)}, bf16[2,128,384]{2,1,0:T(8,128)(2,1)S(1)}, u32[]{:S(2)}, u32[]{:S(2)}) collective-permute-start(bf16[2,128,384]{2,1,0:T(8,128)(2,1)S(1)} %get-tuple-element.25), channel_id=1, source_target_pairs={{0,128},{4,132},{8,136},{12,140},{16,144},{20,148},{24,152},{28,15... | collective-permute-start | bytes 589832 | tf_op jit(solution)/shard_map/ppermute | solution.py:14
  13.9 1.3 %collective-permute-start.3 = (bf16[2,128,384]{2,1,0:T(8,128)(2,1)S(1)}, bf16[2,128,384]{2,1,0:T(8,128)(2,1)S(1)}, u32[]{:S(2)}, u32[]{:S(2)}) collective-permute-start(bf16[2,128,384]{2,1,0:T(8,128)(2,1)S(1)} %get-tuple-element.25), channel_id=1, source_target_pairs={{128,0},{132,4},{136,8},{140,12},{144,16},{148,20},{152,24},{156,2... | collective-permute-start | bytes 589832 | tf_op jit(solution)/shard_map/ppermute | solution.py:14
  15.2 1.4 %fusion.59 = (s32[1,1]{1,0:T(1,128)}, s32[1,1]{1,0:T(1,128)}, s32[1,1]{1,0:T(1,128)}, s32[1,1]{1,0:T(1,128)}) fusion(s32[1,4]{1,0:T(1,128)} %param.11), kind=kLoop, calls=%fused_computation.108 | loop fusion | bytes 32 | tf_op jit(solution)/shard_map/slice | solution.py:52
  19.3 0.1 stack.37
  19.5 1.0 %copy.22 = bf16[128,384]{0,1:T(8,128)(2,1)S(1)} copy(bf16[128,384]{1,0:T(8,128)(2,1)} %param.9) | data formatting | bytes 196608 | tf_op args[3]
  20.6 8.5 %collective-permute-done.3 = bf16[2,128,384]{2,1,0:T(8,128)(2,1)S(1)} collective-permute-done((bf16[2,128,384]{2,1,0:T(8,128)(2,1)S(1)}, bf16[2,128,384]{2,1,0:T(8,128)(2,1)S(1)}, u32[]{:S(2)}, u32[]{:S(2)}) %collective-permute-start.3) | collective-permute-done | bytes 196640 | tf_op jit(solution)/shard_map/ppermute | solution.py:14
  29.2 0.1 slice_bitcast_fusion
  29.3 0.8 copy-done
  30.1 0.3 fusion.60
  30.3 0.3 fusion.61
  30.6 0.3 fusion.62
  30.9 0.1 fusion.23
  31.0 0.1 fusion.21
  31.2 0.3 convolution_convert_fusion
  31.5 0.3 convolution_convert_fusion.1
  31.8 0.1 fusion.19
  32.0 0.3 convolution_convert_fusion.2
  32.3 0.1 multiply_reduce_fusion
  32.4 12.9 %psum.7 = f32[128]{0:T(128)S(1)} all-reduce(f32[128]{0:T(128)S(1)} %get-tuple-element.15), channel_id=1, replica_groups=mesh['band'=128,'head'=4] {'head'}, use_global_device_ids=true, to_apply=%region_9.10 | all-reduce | flops 128 | bytes 1024 | tf_op jit(solution)/shard_map/psum | solution.py:82
  45.3 9.9 %all-gather.1 = f32[4,1,128]{2,1,0:T(1,128)S(1)} all-gather(f32[1,1,128]{2,1,0:T(1,128)S(1)} %bitcast.48), channel_id=2, replica_groups=mesh['band'=128,'head'=4] {'head'}, dimensions={0}, use_global_device_ids=true | all-gather | bytes 2560 | tf_op jit(solution)/shard_map/all_gather | solution.py:77
  55.2 0.1 subtract_convert_fusion
  55.4 0.2 fusion.8
  55.6 0.3 fusion.11
  55.9 0.2 convolution_multiply_fusion.1
  56.1 0.2 fusion.7
  56.3 0.3 fusion.10
  56.6 0.2 convolution_multiply_fusion.2
  56.8 0.2 fusion.49
  57.0 0.2 fusion.52
  57.2 0.2 fusion.46
  57.4 0.2 fusion.9
  57.6 0.2 convolution_multiply_fusion
  57.7 0.1 maximum_bitcast_fusion
  57.9 0.2 fusion
  58.0 0.8 %fusion.58 = (bf16[2,128,384]{2,1,0:T(8,128)(2,1)}, bf16[2,128,384]{2,1,0:T(8,128)(2,1)}, bf16[2,128,384]{2,1,0:T(8,128)(2,1)S(1)}, bf16[2,128,384]{2,1,0:T(8,128)(2,1)S(1)}) fusion(bf16[2,640,384]{2,1,0:T(8,128)(2,1)S(1)} %fusion), kind=kLoop, calls=%fused_computation.107 | loop fusion | bytes 1572864 | tf_op jit(solution)/shard_map/slice | solution.py:111
  58.9 1.3 %collective-permute-start.4 = (bf16[2,128,384]{2,1,0:T(8,128)(2,1)}, bf16[2,128,384]{2,1,0:T(8,128)(2,1)S(1)}, u32[]{:S(2)}, u32[]{:S(2)}) collective-permute-start(bf16[2,128,384]{2,1,0:T(8,128)(2,1)} %get-tuple-element.17), channel_id=1, source_target_pairs={{128,0},{132,4},{136,8},{140,12},{144,16},{148,20},{152,24},{156,2... | collective-permute-start | bytes 589832 | tf_op jit(solution)/shard_map/ppermute | solution.py:14
  60.2 5.5 %collective-permute-start.7 = (bf16[2,128,384]{2,1,0:T(8,128)(2,1)}, bf16[2,128,384]{2,1,0:T(8,128)(2,1)S(1)}, u32[]{:S(2)}, u32[]{:S(2)}) collective-permute-start(bf16[2,128,384]{2,1,0:T(8,128)(2,1)} %get-tuple-element.18), channel_id=1, source_target_pairs={{0,128},{4,132},{8,136},{12,140},{16,144},{20,148},{24,152},{28,15... | collective-permute-start | bytes 589832 | tf_op jit(solution)/shard_map/ppermute | solution.py:14
  65.6 5.0 %collective-permute-start.6 = (bf16[2,128,384]{2,1,0:T(8,128)(2,1)S(1)}, bf16[2,128,384]{2,1,0:T(8,128)(2,1)}, u32[]{:S(2)}, u32[]{:S(2)}) collective-permute-start(bf16[2,128,384]{2,1,0:T(8,128)(2,1)S(1)} %get-tuple-element.19), channel_id=1, source_target_pairs={{0,64},{4,68},{8,72},{12,76},{16,80},{20,84},{24,88},{28,92},{32,9... | collective-permute-start | bytes 589832 | tf_op jit(solution)/shard_map/ppermute | solution.py:14
  70.6 1.3 %collective-permute-start.5 = (bf16[2,128,384]{2,1,0:T(8,128)(2,1)S(1)}, bf16[2,128,384]{2,1,0:T(8,128)(2,1)}, u32[]{:S(2)}, u32[]{:S(2)}) collective-permute-start(bf16[2,128,384]{2,1,0:T(8,128)(2,1)S(1)} %get-tuple-element.20), channel_id=1, source_target_pairs={{64,0},{68,4},{72,8},{76,12},{80,16},{84,20},{88,24},{92,28},{96,3... | collective-permute-start | bytes 589832 | tf_op jit(solution)/shard_map/ppermute | solution.py:14
  71.9 0.3 fusion.12
  72.1 0.8 copy.32
  72.9 0.8 copy.33
  73.7 4.6 %collective-permute-done.5 = bf16[2,128,384]{2,1,0:T(8,128)(2,1)} collective-permute-done((bf16[2,128,384]{2,1,0:T(8,128)(2,1)S(1)}, bf16[2,128,384]{2,1,0:T(8,128)(2,1)}, u32[]{:S(2)}, u32[]{:S(2)}) %collective-permute-start.5) | collective-permute-done | bytes 196640 | tf_op jit(solution)/shard_map/ppermute | solution.py:14
  78.2 1.1 %fusion.18 = bf16[2,128,384]{2,1,0:T(8,128)(2,1)S(1)} fusion(f32[1,640,384]{2,1,0:T(8,128)S(1)} %get-tuple-element.41, f32[1,640,384]{2,1,0:T(8,128)S(1)} %get-tuple-element.42, bf16[2,128,384]{2,1,0:T(8,128)(2,1)S(1)} %collective-permute-done.7, bf16[2,128,384]{2,1,0:T(8,128)(2,1)} %collective-permute-done.6, ...), kind=kLoop, calls=%fused_computation.40 | loop fusion | flops 983040 | bytes 2949120 | tf_op jit(solution)/shard_map/convert.1
  79.4 0.7 slice_bitcast_fusion.2
  (22 shorter events, 0.5 us)
Async XLA Ops:
  1.6 19.0 %collective-permute-start.2 = (bf16[2,128,384]{2,1,0:T(8,128)(2,1)S(1)}, bf16[2,128,384]{2,1,0:T(8,128)(2,1)S(1)}, u32[]{:S(2)}, u32[]{:S(2)}) collective-permute-start(bf16[2,128,384]{2,1,0:T(8,128)(2,1)S(1)} %get-tuple-element.25), channel_id=1, source_target_pairs={{64,0},{68,4},{72,8},{76,12},{80,16},{84,20},{88,24},{92,28},{96,3... | collective-permute-start | bytes 589832 | tf_op jit(solution)/shard_map/ppermute | solution.py:14
  2.9 17.6 %collective-permute-start.1 = (bf16[2,128,384]{2,1,0:T(8,128)(2,1)S(1)}, bf16[2,128,384]{2,1,0:T(8,128)(2,1)S(1)}, u32[]{:S(2)}, u32[]{:S(2)}) collective-permute-start(bf16[2,128,384]{2,1,0:T(8,128)(2,1)S(1)} %get-tuple-element.25), channel_id=1, source_target_pairs={{0,64},{4,68},{8,72},{12,76},{16,80},{20,84},{24,88},{28,92},{32,9... | collective-permute-start | bytes 589832 | tf_op jit(solution)/shard_map/ppermute | solution.py:14
  7.8 12.6 %collective-permute-start = (bf16[2,128,384]{2,1,0:T(8,128)(2,1)S(1)}, bf16[2,128,384]{2,1,0:T(8,128)(2,1)S(1)}, u32[]{:S(2)}, u32[]{:S(2)}) collective-permute-start(bf16[2,128,384]{2,1,0:T(8,128)(2,1)S(1)} %get-tuple-element.25), channel_id=1, source_target_pairs={{0,128},{4,132},{8,136},{12,140},{16,144},{20,148},{24,152},{28,15... | collective-permute-start | bytes 589832 | tf_op jit(solution)/shard_map/ppermute | solution.py:14
  13.9 15.2 %collective-permute-start.3 = (bf16[2,128,384]{2,1,0:T(8,128)(2,1)S(1)}, bf16[2,128,384]{2,1,0:T(8,128)(2,1)S(1)}, u32[]{:S(2)}, u32[]{:S(2)}) collective-permute-start(bf16[2,128,384]{2,1,0:T(8,128)(2,1)S(1)} %get-tuple-element.25), channel_id=1, source_target_pairs={{128,0},{132,4},{136,8},{140,12},{144,16},{148,20},{152,24},{156,2... | collective-permute-start | bytes 589832 | tf_op jit(solution)/shard_map/ppermute | solution.py:14
  29.2 0.9 %copy-start = (bf16[128,384]{1,0:T(8,128)(2,1)S(1)}, bf16[128,384]{1,0:T(8,128)(2,1)}, u32[]{:S(2)}) copy-start(bf16[128,384]{1,0:T(8,128)(2,1)} %param.6) | copy-start | bytes 294916
  31.5 0.8 copy-start.1
  58.9 14.8 %collective-permute-start.4 = (bf16[2,128,384]{2,1,0:T(8,128)(2,1)}, bf16[2,128,384]{2,1,0:T(8,128)(2,1)S(1)}, u32[]{:S(2)}, u32[]{:S(2)}) collective-permute-start(bf16[2,128,384]{2,1,0:T(8,128)(2,1)} %get-tuple-element.17), channel_id=1, source_target_pairs={{128,0},{132,4},{136,8},{140,12},{144,16},{148,20},{152,24},{156,2... | collective-permute-start | bytes 589832 | tf_op jit(solution)/shard_map/ppermute | solution.py:14
  60.2 13.5 %collective-permute-start.7 = (bf16[2,128,384]{2,1,0:T(8,128)(2,1)}, bf16[2,128,384]{2,1,0:T(8,128)(2,1)S(1)}, u32[]{:S(2)}, u32[]{:S(2)}) collective-permute-start(bf16[2,128,384]{2,1,0:T(8,128)(2,1)} %get-tuple-element.18), channel_id=1, source_target_pairs={{0,128},{4,132},{8,136},{12,140},{16,144},{20,148},{24,152},{28,15... | collective-permute-start | bytes 589832 | tf_op jit(solution)/shard_map/ppermute | solution.py:14
  65.6 8.0 %collective-permute-start.6 = (bf16[2,128,384]{2,1,0:T(8,128)(2,1)S(1)}, bf16[2,128,384]{2,1,0:T(8,128)(2,1)}, u32[]{:S(2)}, u32[]{:S(2)}) collective-permute-start(bf16[2,128,384]{2,1,0:T(8,128)(2,1)S(1)} %get-tuple-element.19), channel_id=1, source_target_pairs={{0,64},{4,68},{8,72},{12,76},{16,80},{20,84},{24,88},{28,92},{32,9... | collective-permute-start | bytes 589832 | tf_op jit(solution)/shard_map/ppermute | solution.py:14
  70.6 7.7 %collective-permute-start.5 = (bf16[2,128,384]{2,1,0:T(8,128)(2,1)S(1)}, bf16[2,128,384]{2,1,0:T(8,128)(2,1)}, u32[]{:S(2)}, u32[]{:S(2)}) collective-permute-start(bf16[2,128,384]{2,1,0:T(8,128)(2,1)S(1)} %get-tuple-element.20), channel_id=1, source_target_pairs={{64,0},{68,4},{72,8},{76,12},{80,16},{84,20},{88,24},{92,28},{96,3... | collective-permute-start | bytes 589832 | tf_op jit(solution)/shard_map/ppermute | solution.py:14
